TPU v7x, 32 devices: a whole 2x2x4 slice. The times are simulated.
32 devices in a mesh: dp: 16 (over z, y, core), tensor: 2 (over x).
Axes of the slice: x: 2, y: 2, z: 4, core: 2. Of those that a mesh axis runs over, the one named last changes fastest.
Arguments:
- tokens: bfloat16 [4096, 1024], P('dp'), may hold values from -24 to 24
- segments: int32 [16, 256], P('dp'), may hold values from 0 to 3, never falling along the last dimension, each value on 1 to 128 neighbouring positions
- positions: int32 [16, 256], P('dp'), may hold values from 0 to 1023
- attn_gain: float32 [1024], replicated, may hold values from 0.5 to 1.5
- w_query: bfloat16 [1024, 2048], P(None, 'tensor'), may hold values from -0.1875 to 0.1875
- key_weight: bfloat16 [1024, 1024], P(None, 'tensor'), may hold values from -0.1875 to 0.1875
- value_weight: bfloat16 [1024, 1024], P(None, 'tensor'), may hold values from -0.1875 to 0.1875
- query_gain: float32 [128], replicated, may hold values from 0.5 to 1.5
- key_gain: float32 [128], replicated, may hold values from 0.5 to 1.5
- w_out: bfloat16 [2048, 1024], P('tensor'), may hold values from -0.75 to 0.75
- ffn_gain: float32 [1024], replicated, may hold values from 0.5 to 1.5
- w_gate: bfloat16 [1024, 3072], P(None, 'tensor'), may hold values from -0.1875 to 0.1875
- w_up: bfloat16 [1024, 3072], P(None, 'tensor'), may hold values from -0.1875 to 0.1875
- w_down: bfloat16 [3072, 1024], P('tensor'), may hold values from -0.109375 to 0.109375
- cotangent: bfloat16 [4096, 1024], P('dp'), may hold values from -6 to 6
Outputs:
- mixed: bfloat16 [4096, 1024], P('dp')
- tokens_grad: bfloat16 [4096, 1024], P('dp')
- attn_gain_grad: float32 [1024], replicated
- w_query_grad: float32 [1024, 2048], P(None, 'tensor')
- w_key_grad: float32 [1024, 1024], P(None, 'tensor')
- w_value_grad: float32 [1024, 1024], P(None, 'tensor')
- query_gain_grad: float32 [128], replicated
- key_gain_grad: float32 [128], replicated
- w_out_grad: float32 [2048, 1024], P('tensor')
- ffn_gain_grad: float32 [1024], replicated
- w_gate_grad: float32 [1024, 3072], P(None, 'tensor')
- w_up_grad: float32 [1024, 3072], P(None, 'tensor')
- w_down_grad: float32 [3072, 1024], P('tensor')
Inputs may be any that keep to these rules, and one draw needn't show every extreme that they name: `segments`: within each packed sequence segment numbers never fall; each document has 1 to 128 tokens and one has exactly that many.
All inputs are finite; a program needn't handle non-finite values.
Results may differ from a plain program's by a relative error of at most 0.013.
Values sent between devices are 32-bit elements; how exact they have to be, the bound alone decides.
A program may use at most 192 MiB of HBM per device.

v0:
```python
import functools
import math

import jax
import jax.numpy as jnp
import numpy as np
from jax import lax
from jax.experimental import pallas as pl
from jax.experimental.pallas import tpu as pltpu
from jax.sharding import PartitionSpec as P

EPS = 1e-06
THETA = 1000000.0
F32 = jnp.float32
BF16 = jnp.bfloat16
MESH = pl.DeviceIdType.MESH
VMEM_BYTES = 32 * 2**20
RESULTS_VMEM_BYTES = 2**20
GROUP = 16
COT, FFN = 0, 1
SHARES = ((2, 2, 2, 3), (4, 4, 4, 4))


PLAN = {
    "A2": [
        ("ring_half", 0),
        ("ring_half", 1),
    ],
    "A5": [
        ("start", "x", COT, 1),
    ],
    "A6": [
        ("ring", COT, 2),
    ],
    "A7": [
        ("start", "x", COT, 2),
        ("start", "x", COT, 3),
        ("start", "x", COT, 4),
        ("ring", FFN, 1),
    ],
    "A10": [
        ("x_done", COT, 1),
        ("start", "x", FFN, 1),
        ("x_done", COT, 2),
        ("start", "x", FFN, 2),
    ],
    (0, 0): [
        ("ring", COT, 3),
    ],
    (0, 1): [
        ("x_done", COT, 3),
        ("start", "x", COT, 5),
    ],
    (2, 0): [
        ("x_done", COT, 4),
        ("start", "x", COT, 6),
    ],
    (2, 1): [
        ("ring", FFN, 2),
        ("gain_sum",),
    ],
    (2, 2): [
        ("sum", 0, 1),
        ("gain", 0),
        ("sum", 1, 1),
        ("x_done", FFN, 1),
        ("start", "x", FFN, 3),
        ("stage", 1),
    ],
    (3, 0): [
        ("ring", COT, 4),
    ],
    (4, 1): [
        ("x_done", FFN, 2),
        ("start", "x", FFN, 4),
    ],
    (5, 2): [
        ("stage", 2),
    ],
    (6, 0): [
        ("ring", FFN, 3),
        ("x_done", COT, 5),
        ("start", "x", FFN, 5),
    ],
    (6, 1): [
        ("x_done", COT, 6),
        ("start", "x", FFN, 6),
    ],
    (7, 0): [
        ("sum", 0, 2),
        ("gain", 1),
    ],
    (8, 2): [
        ("sum", 1, 2),
        ("x_done", FFN, 3),
        ("start", "x", COT, 7),
        ("stage", 3),
    ],
    (9, 0): [
        ("ring", FFN, 4),
    ],
    (10, 1): [
        ("x_done", FFN, 4),
        ("start", "x", FFN, 7),
    ],
    (11, 0): [
        ("sum", 0, 3),
        ("gain", 2),
    ],
    (11, 1): [
        ("stage", 4),
    ],
    (13, 0): [
        ("sum", 1, 3),
        ("x_done", FFN, 5),
        ("start", "part", 2),
    ],
    (14, 1): [
        ("stage", 5),
    ],
    (15, 0): [
        ("sum", 0, 4),
        ("gain", 3),
    ],
    (15, 1): [
        ("x_done", FFN, 6),
        ("start", "part", 3),
    ],
    (17, 0): [
        ("stage", 6),
    ],
    (17, 1): [
        ("sum", 1, 4),
    ],
    (18, 0): [
        ("x_done", COT, 7),
    ],
    (19, 1): [
        ("gather", 0, 1),
    ],
    (20, 0): [
        ("gain", 4),
    ],
    (20, 2): [
        ("x_done", FFN, 7),
        ("gather", 1, 1),
        ("stage", 7),
    ],
    (22, 0): [
        ("gather", 0, 2),
    ],
    (24, 0): [
        ("gather", 1, 2),
        ("tokens",),
        ("gather", 0, 3),
        ("gather", 1, 3),
        ("gather", 0, 4),
        ("mixed",),
        ("gather", 1, 4),
    ],
}


def norm_factor(values):
    return lax.rsqrt(jnp.mean(values * values, axis=-1, keepdims=True) + EPS)


def norm_grad(grad_out, unit_rows, factor, scale_gain):
    scaled = grad_out * scale_gain
    return factor * (scaled - unit_rows * jnp.mean(scaled * unit_rows, axis=-1, keepdims=True))


def rows_dot(leading, trailing):
    return jnp.dot(leading, trailing, preferred_element_type=F32)


def across_rows(leading, trailing):
    return lax.dot_general(
        leading, trailing, (((0,), (0,)), ((), ())), preferred_element_type=F32
    )


def against_rows(leading, trailing):
    return lax.dot_general(
        leading, trailing, (((1,), (1,)), ((), ())), preferred_element_type=F32
    )


def ffn_middle(low_in, cot, wg, wu, wd):
    gate = rows_dot(low_in, wg)
    up = rows_dot(low_in, wu)
    sig = jax.nn.sigmoid(gate)
    silu = gate * sig
    hidden = (silu * up).astype(BF16)
    hidden_grad = against_rows(cot, wd)
    up_grad = (hidden_grad * silu).astype(BF16)
    gate_grad = (hidden_grad * up * sig * (1.0 + gate * (1.0 - sig))).astype(BF16)
    return hidden, gate_grad, up_grad


def shaped(*shape, kind=F32):
    return jax.ShapeDtypeStruct(shape, kind)


class Sizes:
    def __init__(self, dp_size, tokens, w_query, key_weight, query_gain, w_gate):
        self.rows, self.width = tokens
        self.head_width = query_gain[0]
        self.q_cols, self.k_cols = w_query[1], key_weight[1]
        self.heads, self.kv_heads = self.q_cols // self.head_width, self.k_cols // self.head_width
        self.units = w_gate[1]
        self.all_cols = self.q_cols + 2 * self.k_cols
        self.scale = 1.0 / math.sqrt(self.head_width)
        self.group = math.gcd(GROUP, dp_size)
        self.chips = self.group // 2
        self.half = self.chips // 2
        self.share = tuple(tuple(self.width * part // 8 for part in parts) for parts in SHARES)
        self.grad_rows = self.width // 2
        self.grad_cols = self.width + self.all_cols
        self.piece = self.grad_rows // self.chips
        self.streams = 2


def layer_kernel(
    sz,
    tokens_in, cot_in, segments_in, positions_in, inverse_in, attn_gain_in, query_gain_in, key_gain_in,
    ffn_gain_in,
    w_query, key_weight, value_weight, w_out, w_gate, w_up, w_down,
    mixed, tokens_grad, attn_gain_grad, ffn_gain_grad, query_gain_grad, key_gain_grad,
    attn_grads, gate_grads, up_grads, down_grads,
    mine, theirs,
    tokens, cot, segments, positions, inverse, attn_gain, query_gain, key_gain, ffn_gain,
    part, part_theirs, middle_grad, sum_up, sum_down, gain_part, gain_theirs,
    gain_send, gain_recv, gain_slots,
    send_sems, recv_sems, local_sems,
):
    rows, width, head_width = sz.rows, sz.width, sz.head_width
    q_cols, k_cols, units = sz.q_cols, sz.k_cols, sz.units
    n, half, piece = sz.chips, sz.half, sz.piece
    half_units = units // 2
    mid = rows // 2

    device = lax.axis_index("dp")
    base = device // sz.group * sz.group
    core = device % 2
    chip = device % sz.group // 2
    line = chip % 2
    place = chip // 2 + line * (2 * half - 1 - 2 * (chip // 2))
    side = lax.axis_index("tensor")

    def device_at(position):
        position = position % n
        second = position // half
        return base + (2 * (position + second * (2 * half - 1 - 2 * position)) + second) * 2 + core

    forward = {"dp": device_at(place + 1)}
    backward = {"dp": device_at(place + n - 1)}
    sibling = {"dp": base + chip * 2 + 1 - core}
    across = {"tensor": 1 - side}

    barrier = pltpu.get_barrier_semaphore()
    for neighbour in (forward, backward, sibling, across):
        pl.semaphore_signal(barrier, inc=1, device_id=neighbour, device_id_type=MESH)
    small_loads = [
        pltpu.make_async_copy(src, dst, local_sems.at[16 + k])
        for k, (src, dst) in enumerate(
            (
                (cot_in, cot),
                (tokens_in, tokens),
                (attn_gain_in, attn_gain),
                (segments_in, segments),
                (positions_in, positions),
                (inverse_in, inverse),
                (query_gain_in, query_gain),
                (key_gain_in, key_gain),
                (ffn_gain_in, ffn_gain),
            )
        )
    ]
    for load in small_loads:
        load.start()

    book = {}
    waited = set()

    send_of = {}
    before = {}

    def remote(name, src, dst, target, after=None):
        book[name] = (len(book), src, dst, target)
        if after is None:
            send_of[name] = len(set(send_of.values()))
        else:
            send_of[name], before[name] = send_of[after], after

    def made(name):
        index, src, dst, target = book[name]
        return pltpu.make_async_remote_copy(
            src_ref=src, dst_ref=dst, send_sem=send_sems.at[send_of[name]], recv_sem=recv_sems.at[index],
            device_id=target, device_id_type=MESH,
        )

    def sent(*names):
        for name in names:
            if name not in waited:
                made(name).wait_send()
                waited.add(name)

    def start(*names):
        for name in names:
            if name in before:
                sent(before[name])
            made(name).start()

    def arrived(*names):
        for name in names:
            made(name).wait_recv()

    def cols(first, count):
        return pl.ds(pl.multiple_of(first, 128), count)

    def piece_rows(index, first=0, count=piece, base_row=0):
        return pl.ds(pl.multiple_of(base_row + index % n * piece + first, 8), count)

    grad_base = core * sz.grad_rows
    slots = 2 * half
    up_slot = lambda h: 2 * h - 1
    down_slot = lambda h: 2 * h
    last = slots - 1
    up_place = lambda row, first, count: up_grads.at[pl.ds(row * rows, rows), pl.ds(first, count)]
    down_place = lambda row: down_grads.at[pl.ds(row * rows, rows)]
    half_width = width // 2
    gate_place = lambda row: gate_grads.at[pl.ds(row * rows, rows), pl.ds(units - width, width)]
    own = (gate_place(0), gate_place(1))
    in_halves = lambda a, h: a == COT and h <= 2

    def ring_names(a, h):
        count = 2 if in_halves(a, h) else 1
        return [(way, a, h, k) for k in range(count) for way in ("up", "down")]

    for a in (COT, FFN):
        for h in range(1, half + 1):
            share = sz.share[a][h - 1]
            window = cols(side * share, width - share)
            shared = cols(side * (width - share), share)
            up = own[a] if h == 1 else mine.at[a, up_slot(h - 1)]
            down = own[a] if h == 1 else mine.at[a, down_slot(h - 1)]
            first, second = pl.ds(0, mid), pl.ds(mid, mid)
            if h < half:
                for k, part_rows in enumerate((first, second) if in_halves(a, h) else (pl.ds(0, rows),)):
                    to_up = mine.at[a, up_slot(h), part_rows, window]
                    to_down = mine.at[a, down_slot(h), part_rows, window]
                    follows = None if h == 1 else h - 1
                    remote(
                        ("up", a, h, k), up.at[part_rows, window], to_up, forward,
                        follows and ("up", a, follows, k),
                    )
                    remote(
                        ("down", a, h, k), down.at[part_rows, window], to_down, backward,
                        follows and ("down", a, follows, k),
                    )
                of_distance = (up_slot(h), down_slot(h))
            else:
                remote(
                    ("up", a, h, 0), up.at[first, window], mine.at[a, last, first, window], forward,
                    ("up", a, h - 1, 0),
                )
                remote(
                    ("down", a, h, 0), down.at[second, window], mine.at[a, last, second, window],
                    backward, ("down", a, h - 1, 0),
                )
                of_distance = (last,)
            for s in of_distance:
                remote(("x", a, s), mine.at[a, s, :, shared], mine.at[a, s, :, shared], across)
        for s in range(slots):
            remote(("core", a, s), own[a] if s == 0 else mine.at[a, s], theirs.at[a, s], sibling)
    halves = (slice(0, mid), slice(mid, rows))
    for k in range(2):
        for index, at_rows in enumerate(halves):
            at_rows = pl.ds(at_rows.start, mid)
            remote(
                ("part", k, index), part.at[k, at_rows], part_theirs.at[k, at_rows], across
            )
        remote(("part", 2 + k), part.at[1 - k], part_theirs.at[k], across)
    stream_cols = sz.grad_cols // sz.streams
    small = piece // 2
    for s in range(sz.streams):
        c = pl.ds(s * stream_cols, stream_cols)
        for h in range(1, half + 1):
            size, skip = (small, small) if h == 1 else (piece, 0)
            src = attn_grads.at[piece_rows(place + half, 0, small, grad_base), c]
            remote(
                ("su", s, h), src if h == 1 else sum_up.at[h - 2, :, c],
                sum_up.at[h - 1, pl.ds(0, size), c], forward, None if h == 1 else ("su", s, h - 1),
            )
            src = attn_grads.at[piece_rows(place + half, small, small, grad_base), c]
            remote(
                ("sd", s, h), src if h == 1 else sum_down.at[h - 2, :, c],
                sum_down.at[h - 1, pl.ds(skip, size), c], backward, None if h == 1 else ("sd", s, h - 1),
            )
        own_piece = attn_grads.at[piece_rows(place, 0, piece, grad_base), c]
        remote(("cu", s, 0), own_piece, own_piece, sibling)
        for h in range(1, half + 1):
            size, skip = (small, small) if h == half else (piece, 0)
            going_up = attn_grads.at[piece_rows(place + n - h + 1, 0, size, grad_base), c]
            going_down = attn_grads.at[piece_rows(place + h - 1, skip, size, grad_base), c]
            follows = (("su", s, half), ("sd", s, half)) if h == 1 else (("gu", s, h - 1), ("gd", s, h - 1))
            remote(("gu", s, h), going_up, going_up, forward, follows[0])
            remote(("gd", s, h), going_down, going_down, backward, follows[1])
            got_up = attn_grads.at[piece_rows(place + n - h, 0, size, grad_base), c]
            got_down = attn_grads.at[piece_rows(place + h, skip, size, grad_base), c]
            remote(("cu", s, h), got_up, got_up, sibling, ("cu", s, h - 1))
            remote(("cd", s, h), got_down, got_down, sibling, None if h == 1 else ("cd", s, h - 1))
    remote("gain_parts", gain_part, gain_theirs, across)
    remote("gains", gain_send, gain_recv, sibling)
    for h in range(1, half + 1):
        slot = gain_slots.at[(place + n - h + 1) % n]
        remote(("vu", h), slot, slot, forward, None if h == 1 else ("vu", h - 1))
        if h < half:
            slot = gain_slots.at[(place + h - 1) % n]
            remote(("vd", h), slot, slot, backward, None if h == 1 else ("vd", h - 1))

    def ring_step(a, h):
        arrived(*ring_names(a, h))
        if h < half:
            start(*ring_names(a, h + 1))

    def ring_half(k):
        arrived(("up", COT, 1, k), ("down", COT, 1, k))
        start(("up", COT, 2, k), ("down", COT, 2, k))

    def x_start(a, s):
        start(("x", a, s))

    def x_done(a, s):
        arrived(("x", a, s))
        start(("core", a, s))


    def stream(s):
        return pl.ds(s * stream_cols, stream_cols)

    def sum_step(s, h):
        arrived(("su", s, h), ("sd", s, h))
        c = stream(s)
        up_rows = piece_rows(place + half - h, 0, piece, grad_base)
        down_rows = piece_rows(place + n - half + h, 0, piece, grad_base)
        if h == 1:
            sent(("su", s, 1), ("sd", s, 1))
            up, down = attn_grads[up_rows, c], attn_grads[down_rows, c]
            sum_up[0, :small, c] += up[:small]
            sum_up[0, small:, c] = up[small:]
            sum_down[0, :small, c] = down[:small]
            sum_down[0, small:, c] += down[small:]
        elif h < half:
            sum_up[h - 1, :, c] += attn_grads[up_rows, c]
            sum_down[h - 1, :, c] += attn_grads[down_rows, c]
        if h < half:
            start(("su", s, h + 1), ("sd", s, h + 1))
        else:
            own_rows = piece_rows(place, 0, piece, grad_base)
            attn_grads[own_rows, c] += sum_up[h - 1, :, c] + sum_down[h - 1, :, c]
            start(("gu", s, 1), ("gd", s, 1), ("cu", s, 0))

    def gather_step(s, h):
        arrived(("gu", s, h), ("gd", s, h))
        if h < half:
            start(("gu", s, h + 1), ("gd", s, h + 1))
        start(("cu", s, h), ("cd", s, h))

    def finish_tokens():
        arrived(("part", 2))
        grad = part[1] + part_theirs[0]
        value = tokens[...].astype(F32)
        factor = norm_factor(value)
        unit = value * factor
        tokens_grad[...] = (
            middle_grad[...] + norm_grad(grad, unit, factor, attn_gain[...])
        ).astype(BF16)

    def finish_mixed():
        arrived(("part", 3))
        mixed[...] = (part[0] + part_theirs[1]).astype(BF16)

    def gain_sum():
        arrived("gain_parts")
        gain_send[...] = gain_part[...] + gain_theirs[...]
        start("gains")

    def gain_first():
        arrived("gains")
        gain_slots[place] = gain_send[...] + gain_recv[...]
        start(("vu", 1), ("vd", 1))

    def gain_step(h):
        arrived(("vu", h))
        if h < half:
            arrived(("vd", h))
            start(("vu", h + 1))
            if h + 1 < half:
                start(("vd", h + 1))
        else:
            total = gain_slots[0]
            for chip_at in range(1, n):
                total = total + gain_slots[chip_at]
            attn_gain_grad[...] = total[0:1, :]
            ffn_gain_grad[...] = total[1:2, :]
            query_gain_grad[...] = total[2:3, :head_width]
            key_gain_grad[...] = total[2:3, head_width : 2 * head_width]

    def stage(slot):
        arrived(("core", COT, slot), ("core", FFN, slot))
        for copy in stage_copies(slot, False):
            copy.start()

    scoped = {}

    def stage_copies(slot, first):
        staged = scoped["staged"]
        copies = []
        for a in (COT, FFN):
            src = own[a] if first else mine.at[a, slot]
            copies.append(pltpu.make_async_copy(src, staged.at[a, 0], local_sems.at[9 + 2 * a]))
            copies.append(
                pltpu.make_async_copy(theirs.at[a, slot], staged.at[a, 1], local_sems.at[10 + 2 * a])
            )
        return copies

    def gain_event(h):
        if h == 0:
            gain_first()
        else:
            gain_step(h)

    actions = {
        "ring": ring_step,
        "ring_half": ring_half,
        "start": lambda *name: start(name),
        "x_done": x_done,
        "sum": sum_step,
        "gather": gather_step,
        "stage": stage,
        "gain_sum": gain_sum,
        "tokens": finish_tokens,
        "gain": gain_event,
        "mixed": finish_mixed,
    }

    def run(when):
        for event in PLAN.get(when, ()):
            actions[event[0]](*event[1:])

    group = q_cols // k_cols
    other_half = lambda count: cols((1 - core) * count, count)
    own_half = lambda count: cols(core * count, count)

    block = k_cols
    q_blocks, unit_blocks = q_cols // block, units // block
    at_k, at_v, at_o = q_blocks, q_blocks + 1, q_blocks + 2

    half_down = down_grads.at[pl.ds(pl.multiple_of(core * half_units, 8), half_units)]
    outs = (gate_grads.at[:, own_half(half_units)], up_grads.at[:, own_half(half_units)], half_down)
    for k, out in enumerate(outs):
        remote(("out", k), out, out, sibling)

    q_lin, k_lin = up_place(0, 0, q_cols), up_place(0, q_cols, k_cols)
    ctx_send, ctx_recv = up_place(1, 0, q_cols // 2), up_place(1, q_cols // 2, q_cols // 2)
    cosine, sine = up_place(1, q_cols, head_width), up_place(1, q_cols + head_width, head_width)
    attn_send, attn_recv = up_place(2, 0, half_width), up_place(2, half_width, half_width)
    mask = up_place(3, 0, rows)
    lows, low_recvs = (down_place(0), down_place(1)), (down_place(2), down_place(3))
    branch, branch_recv = down_place(4), down_place(5)
    deep = width // rows
    middle = gate_place(2)

    def probs_of(head):
        return gate_grads.at[pl.ds(head % deep * rows, rows), pl.ds(head // deep * rows, rows)]

    remote("ctx", ctx_send, ctx_recv, sibling)
    remote("attn", attn_send, attn_recv, sibling)
    remote("branch", branch, branch_recv, sibling)
    for k in range(2):
        remote(("low", k), lows[k], low_recvs[k], sibling)

    def first_phase(
        bank, wd, q_low, k_low, v_low, context, ffn_low, hidden, context_grad, attn_low, branch_low
    ):
        def load(src, dst, index):
            copy = pltpu.make_async_copy(src, dst, local_sems.at[index])
            copy.start()
            return copy

        def block_of(weights, index):
            return weights.at[:, pl.ds(index * block, block)]

        def load_projections():
            order = [(w_query, i) for i in range(q_blocks)] + [(key_weight, 0), (value_weight, 0)]
            return [load(block_of(w, i), bank.at[k], k) for k, (w, i) in enumerate(order)]

        def load_out():
            count = width // block
            return [load(block_of(w_out, i), bank.at[at_o + i], at_o + i) for i in range(count)]

        def load_ffn():
            order = [(w, i) for w in (w_gate, w_up) for i in range(unit_blocks)]
            return [load(block_of(w, i), bank.at[k], k) for k, (w, i) in enumerate(order)]

        loads = load_projections()

        def head_norm(lin, gain):
            return lin * norm_factor(lin) * gain[...]

        def turned(lin, gain, at_rows):
            normed = head_norm(lin, gain)
            swapped = pltpu.roll(normed, head_width // 2, 1)
            return (normed * cosine[at_rows] + swapped * sine[at_rows]).astype(BF16)

        def turned_back(grad, lin, gain):
            back = grad * cosine[...] - pltpu.roll(grad, head_width // 2, 1) * sine[...]
            factor = norm_factor(lin)
            unit = lin * factor
            return (
                norm_grad(back, unit, factor, gain[...]).astype(BF16),
                jnp.sum(back * unit, axis=0, keepdims=True),
            )

        small_loads[0].wait()
        own[COT][...] = cot[...].astype(F32)
        pl.semaphore_wait(barrier, 4)
        start(*ring_names(COT, 1), ("core", COT, 0))

        for small in small_loads[1:]:
            small.wait()
        resid = tokens[...].astype(F32)
        attn_in = (resid * norm_factor(resid) * attn_gain[...]).astype(BF16)
        attn_low[...] = attn_in
        attn_send[...] = attn_low[:, other_half(width // 2)].astype(F32)
        start("attn")

        def down_rows(row):
            return jnp.broadcast_to(row.astype(F32), (head_width, rows)).T

        segment_rows = jnp.concatenate([down_rows(segments[...])] * (rows // head_width), 1)
        same = segment_rows == jnp.broadcast_to(segments[...].astype(F32), (rows, rows))
        row_at = lax.broadcasted_iota(jnp.int32, (rows, rows), 0)
        column_at = lax.broadcasted_iota(jnp.int32, (rows, rows), 1)
        mask[...] = jnp.where(same & (row_at >= column_at), 1.0, 0.0)
        angles = down_rows(positions[...]) * inverse[...]
        lane = lax.broadcasted_iota(jnp.int32, (rows, head_width), 1)
        cosine[...] = jnp.cos(angles)
        sine[...] = jnp.where(lane < head_width // 2, -1.0, 1.0) * jnp.sin(angles)
        for i in range(q_blocks):
            loads[i].wait()
            q_lin[:, i * block : (i + 1) * block] = rows_dot(attn_in, bank[i])
        loads[at_k].wait()
        k_lin[...] = rows_dot(attn_in, bank[at_k])
        loads[at_v].wait()
        v_low[...] = rows_dot(attn_in, bank[at_v]).astype(BF16)
        loads += load_out()
        run("A1")
        for kv in range(sz.kv_heads):
            kv_at = slice(kv * head_width, (kv + 1) * head_width)
            k_low[:, kv_at] = turned(k_lin[:, kv_at], key_gain, slice(0, rows))
        for index, at_rows in enumerate(halves):
            seen = at_rows.stop
            for head in range(sz.heads):
                at = slice(head * head_width, (head + 1) * head_width)
                kv_at = slice(head // group * head_width, (head // group + 1) * head_width)
                queries = turned(q_lin[at_rows, at], query_gain, at_rows)
                q_low[at_rows, at] = queries
                scores = against_rows(queries, k_low[:seen, kv_at]) * sz.scale
                scores = jnp.where(mask[at_rows, :seen] > 0, scores, -1e30)
                raised = jnp.exp(scores - jnp.max(scores, axis=-1, keepdims=True))
                prob = raised / jnp.sum(raised, axis=-1, keepdims=True)
                place_of = probs_of(head)
                place_of[at_rows, :seen] = prob
                if seen < rows:
                    place_of[at_rows, seen:] = jnp.zeros((mid, rows - seen), F32)
                context[at_rows, at] = rows_dot(prob.astype(BF16), v_low[:seen, kv_at]).astype(BF16)
            for i in range(width // block):
                if index == 0:
                    loads[at_o + i].wait()
                at = slice(i * block, (i + 1) * block)
                part[0, at_rows, at] = rows_dot(context[at_rows], bank[at_o + i])
            start(("part", 0, index))
        ctx_send[...] = context[:, other_half(q_cols // 2)].astype(F32)
        start("ctx")
        loads = load_ffn()
        down_load = load(w_down, wd, 15)
        for index, at_rows in enumerate(halves):
            run("A2" if index == 0 else "A3")
            arrived(("part", 0, index))
            value = tokens[at_rows].astype(F32) + (part[0, at_rows] + part_theirs[0, at_rows])
            middle[at_rows] = value
            low_rows = (value * norm_factor(value) * ffn_gain[...]).astype(BF16)
            ffn_low[at_rows] = low_rows
            own[FFN][at_rows] = low_rows.astype(F32)
            if index == 0:
                down_load.wait()
                for load_of in loads:
                    load_of.wait()
            else:
                start(*ring_names(FFN, 1), ("core", FFN, 0))
                run("A4")
            for i in range(unit_blocks):
                at = slice(i * block, (i + 1) * block)
                wg, wu = bank[i], bank[unit_blocks + i]
                low_hidden, gate_grad, up_grad = ffn_middle(low_rows, cot[at_rows], wg, wu, wd[at])
                hidden[at_rows, at] = low_hidden
                term = against_rows(gate_grad, wg) + against_rows(up_grad, wu)
                if i == 0:
                    part[1, at_rows] = term
                else:
                    part[1, at_rows] += term
            start(("part", 1, index))
        loads = load_projections() + load_out()
        run("A5")
        sent(("part", 0, 0), ("part", 0, 1))
        part[0] = rows_dot(hidden[...], wd[...]) + 0.5 * middle[...]

        for index, at_rows in enumerate(halves):
            run("A6" if index == 0 else "A7")
            arrived(("part", 1, index))
            grad = part[1, at_rows] + part_theirs[1, at_rows]
            value = middle[at_rows]
            factor = norm_factor(value)
            unit = value * factor
            total = cot[at_rows].astype(F32) + norm_grad(grad, unit, factor, ffn_gain[...])
            middle_grad[at_rows] = total
            branch_low[at_rows] = total.astype(BF16)
            branch[at_rows] = total.astype(BF16).astype(F32)
            gain_term = jnp.sum(grad * unit, axis=0, keepdims=True)
            gain_part[1:2, :] = gain_term if index == 0 else 0.5 * (gain_part[1:2, :] + gain_term)
        start("branch")
        run("A8")
        for load_of in loads:
            load_of.wait()
        context_grad[...] = sum(
            against_rows(branch_low[:, i * block : (i + 1) * block], bank[at_o + i])
            for i in range(width // block)
        ).astype(BF16)
        q_total = jnp.zeros((1, head_width), F32)
        k_total = jnp.zeros((1, head_width), F32)
        for kv in range(sz.kv_heads):
            kv_at = slice(kv * head_width, (kv + 1) * head_width)
            keys, values = k_low[:, kv_at], v_low[:, kv_at]
            keys_grad = values_grad = 0.0
            for member in range(group):
                head = kv * group + member
                at = slice(head * head_width, (head + 1) * head_width)
                head_grad = context_grad[:, at]
                prob = probs_of(head)[...]
                prob_grad = against_rows(head_grad, values)
                values_grad += across_rows(prob.astype(BF16), head_grad)
                inner = jnp.sum(prob * prob_grad, axis=-1, keepdims=True)
                score_grad = (prob * (prob_grad - inner)).astype(BF16)
                queries_grad = rows_dot(score_grad, keys) * sz.scale
                keys_grad += across_rows(score_grad, q_low[:, at])
                head_low, head_total = turned_back(queries_grad, q_lin[:, at], query_gain)
                lows[0][:, at] = head_low.astype(F32)
                q_total += head_total
            head_low, head_total = turned_back(keys_grad * sz.scale, k_lin[:, kv_at], key_gain)
            k_total += head_total
            lows[1][:, kv_at] = head_low.astype(F32)
            at = k_cols + kv * head_width
            lows[1][:, at : at + head_width] = values_grad.astype(BF16).astype(F32)
        start(("low", 0), ("low", 1))
        run("A9")
        half_rows = pl.ds(pl.multiple_of(grad_base, 8), sz.grad_rows)
        arrived("ctx", "branch")
        for i in range(width // block):
            at = slice(i * block, (i + 1) * block)
            attn_grads[half_rows, at] = across_rows(
                context[:, own_half(q_cols // 2)], branch[:, at].astype(BF16)
            ) + across_rows(ctx_recv[...].astype(BF16), branch_recv[:, at].astype(BF16))
        arrived("attn", ("low", 0), ("low", 1))
        for k in range(2):
            for i in range(width // block):
                at = slice(i * block, (i + 1) * block)
                first = (k + 1) * width + i * block
                attn_grads[half_rows, first : first + block] = across_rows(
                    attn_low[:, own_half(width // 2)], lows[k][:, at].astype(BF16)
                ) + across_rows(attn_recv[...].astype(BF16), low_recvs[k][:, at].astype(BF16))
        for s in range(sz.streams):
            start(("su", s, 1), ("sd", s, 1))
        sent(("part", 1, 0), ("part", 1, 1))
        part[1] = sum(
            against_rows(
                lows[i // q_blocks][:, i % q_blocks * block : (i % q_blocks + 1) * block].astype(BF16),
                bank[i],
            )
            for i in range(at_o)
        )
        value = tokens[...].astype(F32)
        unit = value * norm_factor(value)
        gain_part[0:1, :] = jnp.sum(part[1] * unit, axis=0, keepdims=True)
        gain_part[2:, :] = jnp.zeros((6, width), F32)
        gain_part[2:3, :head_width] = q_total
        gain_part[2:3, head_width : 2 * head_width] = k_total
        start("gain_parts")
        run("A10")
        sent("ctx", "attn", "branch", ("low", 0), ("low", 1))

    pl.run_scoped(
        first_phase,
        pltpu.VMEM((max(at_o + width // block, 2 * unit_blocks), width, block), BF16),
        pltpu.VMEM(w_down.shape, BF16),
        pltpu.VMEM((rows, q_cols), BF16),
        pltpu.VMEM((rows, k_cols), BF16),
        pltpu.VMEM((rows, k_cols), BF16),
        pltpu.VMEM((rows, q_cols), BF16),
        pltpu.VMEM((rows, width), BF16),
        pltpu.VMEM((rows, units), BF16),
        pltpu.VMEM((rows, q_cols), BF16),
        pltpu.VMEM((rows, width), BF16),
        pltpu.VMEM((rows, width), BF16),
    )

    def second_phase(
        wg, wu, wd, staged, ffn_low, ffn_turned, cot_low
    ):
        scoped["staged"] = staged
        weight_loads = [
            pltpu.make_async_copy(src, dst, local_sems.at[i])
            for i, (src, dst) in enumerate(
                (
                    (w_gate.at[:, own_half(half_units)], wg),
                    (w_up.at[:, own_half(half_units)], wu),
                    (w_down.at[pl.ds(pl.multiple_of(core * half_units, 8), half_units)], wd),
                )
            )
        ]
        for load in weight_loads:
            load.start()

        for a in (COT, FFN):
            sent(*ring_names(a, 1), ("core", a, 0))
        arrived(("core", COT, 0), ("core", FFN, 0))
        for copy in stage_copies(0, True):
            copy.start()
        for load in weight_loads:
            load.wait()
        chunks = 3
        size = half_units // chunks
        def step(i, _):
            slot, j = i // chunks, i % chunks

            @pl.when(j == 0)
            def _():
                for copy in stage_copies(slot, False):
                    copy.wait()
                for lane in range(2):
                    here = pl.ds(lane * rows, rows)
                    low_block = staged[FFN, lane].astype(BF16)
                    ffn_low[here] = low_block
                    ffn_turned[:, lane * rows : (lane + 1) * rows] = low_block.T
                    cot_low[here] = staged[COT, lane].astype(BF16)

            def events(part_of_step):
                for when in PLAN:
                    if isinstance(when, tuple) and when[0] < chunks * slots and when[1] == part_of_step:

                        @pl.when(i == when[0])
                        def _():
                            run(when)

            events(0)
            at_units = pl.ds(pl.multiple_of(j * size, 128), size)
            hidden, gate_grad, up_grad = ffn_middle(
                ffn_low[...], cot_low[...], wg[:, at_units], wu[:, at_units], wd[at_units]
            )
            events(1)
            down = across_rows(hidden, cot_low[...])
            gate = rows_dot(ffn_turned[...], gate_grad)
            up = rows_dot(ffn_turned[...], up_grad)

            grad_units = core * half_units + j * size
            grad_cols = pl.ds(pl.multiple_of(grad_units, 128), size)

            @pl.when(slot == 0)
            def _():
                gate_grads[:, grad_cols] = gate
                up_grads[:, grad_cols] = up
                down_grads[grad_cols] = down

            @pl.when(slot > 0)
            def _():
                gate_grads[:, grad_cols] += gate
                up_grads[:, grad_cols] += up
                down_grads[grad_cols] += down

            events(2)
            return 0

        lax.fori_loop(0, chunks * slots, step, 0)
        for k in range(3):
            start(("out", k))
        run((chunks * slots, 0))
        for k in range(3):
            arrived(("out", k))

    pl.run_scoped(
        second_phase,
        pltpu.VMEM((width, half_units), BF16),
        pltpu.VMEM((width, half_units), BF16),
        pltpu.VMEM((half_units, width), BF16),
        pltpu.VMEM((2, 2, rows, width), F32),
        pltpu.VMEM((2 * rows, width), BF16),
        pltpu.VMEM((width, 2 * rows), BF16),
        pltpu.VMEM((2 * rows, width), BF16),
    )
    for s in range(sz.streams):
        for h in range(half + 1):
            arrived(("cu", s, h))
            if h:
                arrived(("cd", s, h))
    for name in book:
        if name not in waited:
            made(name).wait_send()


def results_kernel(*refs):
    count = 10
    held, places, sems = refs[:count], refs[count:-1], refs[-1]
    moves = list(zip(held[:-1], places))
    first = 0
    for dst in places[count - 1 :]:
        moves.append((held[-1].at[:, pl.ds(first, dst.shape[1])], dst))
        first += dst.shape[1]
    copies = [
        pltpu.make_async_copy(src, dst, sems.at[k]) for k, (src, dst) in enumerate(moves)
    ]
    for copy in copies:
        copy.start()
    for copy in copies:
        copy.wait()


def over_groups(sz, dp_size, values):
    step = sz.group
    while step < dp_size:
        values = values + lax.ppermute(values, "dp", [(d, d ^ step) for d in range(dp_size)])
        step *= 2
    return values


def per_device(
    dp_size,
    tokens,
    segments,
    positions,
    attn_gain,
    w_query,
    key_weight,
    value_weight,
    query_gain,
    key_gain,
    w_out,
    ffn_gain,
    w_gate,
    w_up,
    w_down,
    cotangent,
):
    sz = Sizes(dp_size, tokens.shape, w_query.shape, key_weight.shape, query_gain.shape, w_gate.shape)
    rows, width, head_width, half = sz.rows, sz.width, sz.head_width, sz.half
    q_cols, k_cols = sz.q_cols, sz.k_cols
    lanes = np.arange(head_width) % (head_width // 2)
    inverse = (THETA ** (-2.0 * lanes / head_width)).astype(np.float32)[None]
    vmem = pl.BlockSpec(memory_space=pltpu.VMEM)
    anywhere = pl.BlockSpec(memory_space=pl.ANY)
    slots = 2 * half
    transfers, sends = 123, 62
    mixed, tokens_grad, *others = pl.pallas_call(
        functools.partial(layer_kernel, sz),
        out_shape=[
            pltpu.VMEM((rows, width), BF16),
            pltpu.VMEM((rows, width), BF16),
            pltpu.VMEM((1, width), F32),
            pltpu.VMEM((1, width), F32),
            pltpu.VMEM((1, head_width), F32),
            pltpu.VMEM((1, head_width), F32),
            pltpu.VMEM((width, sz.grad_cols), F32),
            pltpu.VMEM(w_gate.shape, F32),
            pltpu.VMEM(w_up.shape, F32),
            pltpu.VMEM(w_down.shape, F32),
            shaped(2, slots, rows, width),
            shaped(2, slots, rows, width),
        ],
        in_specs=[anywhere] * 16,
        out_specs=[vmem] * 10 + [anywhere] * 2,
        scratch_shapes=[
            pltpu.VMEM((rows, width), BF16),
            pltpu.VMEM((rows, width), BF16),
            pltpu.VMEM((1, rows), jnp.int32),
            pltpu.VMEM((1, rows), jnp.int32),
            pltpu.VMEM((1, head_width), F32),
            pltpu.VMEM((1, width), F32),
            pltpu.VMEM((1, head_width), F32),
            pltpu.VMEM((1, head_width), F32),
            pltpu.VMEM((1, width), F32),
            pltpu.VMEM((2, rows, width), F32),
            pltpu.VMEM((2, rows, width), F32),
            pltpu.VMEM((rows, width), F32),
            pltpu.VMEM((half, sz.piece, sz.grad_cols), F32),
            pltpu.VMEM((half, sz.piece, sz.grad_cols), F32),
            pltpu.VMEM((8, width), F32),
            pltpu.VMEM((8, width), F32),
            pltpu.VMEM((8, width), F32),
            pltpu.VMEM((8, width), F32),
            pltpu.VMEM((sz.chips, 8, width), F32),
            pltpu.SemaphoreType.DMA((sends,)),
            pltpu.SemaphoreType.DMA((transfers,)),
            pltpu.SemaphoreType.DMA((25,)),
        ],
        compiler_params=pltpu.CompilerParams(
            collective_id=0, has_side_effects=True, vmem_limit_bytes=VMEM_BYTES
        ),
    )(
        tokens, cotangent, segments, positions, jnp.asarray(inverse), attn_gain[None], query_gain[None], key_gain[None],
        ffn_gain[None], w_query, key_weight, value_weight, w_out, w_gate, w_up, w_down,
    )
    sums = [over_groups(sz, dp_size, values) for values in others[:-2]]
    attn_grads = sums.pop(4)
    results = [mixed, tokens_grad, *sums, attn_grads]
    places = [shaped(*v.shape, kind=v.dtype) for v in results[:-1]]
    places += [shaped(*v.shape) for v in (w_out, w_query, key_weight, value_weight)]
    (
        mixed, tokens_grad, attn_gain_grad, ffn_gain_grad, query_gain_grad, key_gain_grad,
        w_gate_grad, w_up_grad, w_down_grad, w_out_grad, w_query_grad, w_key_grad, w_value_grad,
    ) = pl.pallas_call(
        results_kernel,
        out_shape=places,
        in_specs=[anywhere] * len(results),
        out_specs=[anywhere] * len(places),
        scratch_shapes=[pltpu.SemaphoreType.DMA((len(places),))],
        compiler_params=pltpu.CompilerParams(vmem_limit_bytes=RESULTS_VMEM_BYTES),
    )(*[pltpu.with_memory_space_constraint(values, pltpu.VMEM) for values in results])
    return (
        mixed,
        tokens_grad,
        attn_gain_grad[0],
        w_query_grad,
        w_key_grad,
        w_value_grad,
        query_gain_grad[0],
        key_gain_grad[0],
        w_out_grad,
        ffn_gain_grad[0],
        w_gate_grad,
        w_up_grad,
        w_down_grad,
    )


def solution(mesh):
    def layer(*arrays):
        return per_device(mesh.shape["dp"], *arrays)

    return jax.shard_map(
        layer,
        mesh=mesh,
        in_specs=(
            P("dp", None),
            P("dp", None),
            P("dp", None),
            P(),
            P(None, "tensor"),
            P(None, "tensor"),
            P(None, "tensor"),
            P(),
            P(),
            P("tensor", None),
            P(),
            P(None, "tensor"),
            P(None, "tensor"),
            P("tensor", None),
            P("dp", None),
        ),
        out_specs=(
            P("dp", None),
            P("dp", None),
            P(),
            P(None, "tensor"),
            P(None, "tensor"),
            P(None, "tensor"),
            P(),
            P(),
            P("tensor", None),
            P(),
            P(None, "tensor"),
            P(None, "tensor"),
            P("tensor", None),
        ),
        check_vma=False,
    )
```

profile of v0, /device:TPU:0, one launch (start us, length us, event | category | flops | bytes accessed | tf_op | source)
XLA Modules:
  0.0 237.6 jit_solution(15413549466518350415)
XLA Ops:
  0.7 226.0 %shard_map.255 = (bf16[256,1024]{1,0:T(8,128)(2,1)S(1)}, bf16[256,1024]{1,0:T(8,128)(2,1)S(1)}, f32[1,1024]{1,0:T(1,128)S(1)}, f32[1,1024]{1,0:T(1,128)S(1)}, f3...) custom-call(bf16[256,1024]{1,0:T(8,128)(2,1)} %tokens_in.1, ...), custom_call_target="tpu_custom_call" | custom-call | tf_op jit(solution)/shard_map/pallas_call | solution.py:974
  226.6 10.8 %shard_map.256 = (bf16[256,1024]{1,0:T(8,128)(2,1)}, bf16[256,1024]{1,0:T(8,128)(2,1)}, f32[1,1024]{1,0:T(1,128)}, f32[1,1024]{1,0:T(1,128)}, f32[1,128]{1,0:T(1...) custom-call(bf16[256,1024]{1,0:T(8,128)(2,1)S(1)} %get-tuple-element, ...), custom_call_target="tpu_custom_call" | custom-call | tf_op jit(solution)/shard_map/pallas_call | solution.py:1031
where the time goes:
time: 238 us
  Pallas kernels  237 us (100%)
    pallas_call x1, Pallas kernels, per_device(): pl.pallas_call(functools.partial(layer_kernel, sz), out_shape=[pltpu.VMEM...  226 us
    pallas_call x1, Pallas kernels, per_device(): pl.pallas_call(results_kernel, out_shape=places, in_specs=[anywhere] * le...  10.8 us

commit v1 on v0

--- a/solution.py
+++ b/solution.py
@@ -337,6 +337,11 @@
     def ring_names(a, h):
         count = 2 if in_halves(a, h) else 1
         return [(way, a, h, k) for k in range(count) for way in ("up", "down")]
+
+    phase = sorted((when for when in PLAN if isinstance(when, str)), key=lambda when: int(when[1:]))
+    steps = sorted(when for when in PLAN if isinstance(when, tuple))
+    passed = [e[1:] for when in (*phase, *steps) for e in PLAN[when] if e[0] == "x_done"]
+    follows_block = dict(zip(passed[2:], passed))
 
     for a in (COT, FFN):
         for h in range(1, half + 1):
@@ -372,8 +377,12 @@
                 of_distance = (last,)
             for s in of_distance:
                 remote(("x", a, s), mine.at[a, s, :, shared], mine.at[a, s, :, shared], across)
-        for s in range(slots):
-            remote(("core", a, s), own[a] if s == 0 else mine.at[a, s], theirs.at[a, s], sibling)
+    for a, s in [(COT, 0), (FFN, 0), *passed]:
+        last_but_one = follows_block.get((a, s))
+        remote(
+            ("core", a, s), own[a] if s == 0 else mine.at[a, s], theirs.at[a, s], sibling,
+            last_but_one and ("core", *last_but_one),
+        )
     halves = (slice(0, mid), slice(mid, rows))
     for k in range(2):
         for index, at_rows in enumerate(halves):
@@ -970,7 +979,7 @@
     vmem = pl.BlockSpec(memory_space=pltpu.VMEM)
     anywhere = pl.BlockSpec(memory_space=pl.ANY)
     slots = 2 * half
-    transfers, sends = 123, 62
+    transfers, sends = 123, 50
     mixed, tokens_grad, *others = pl.pallas_call(
         functools.partial(layer_kernel, sz),
         out_shape=[

time: 238 us -> 238 us (level)
  no operation moved by 1% of the time
where the time goes in v1:
time: 238 us
  Pallas kernels  237 us (100%)
    pallas_call x1, Pallas kernels, per_device(): pl.pallas_call(functools.partial(layer_kernel, sz), out_shape=[pltpu.VMEM...  226 us
    pallas_call x1, Pallas kernels, per_device(): pl.pallas_call(results_kernel, out_shape=places, in_specs=[anywhere] * le...  10.8 us

profile of v1, /device:TPU:0, one launch (start us, length us, event | category | flops | bytes accessed | tf_op | source)
XLA Modules:
  0.0 237.5 jit_solution(6351157298138709297)
XLA Ops:
  0.7 225.9 %shard_map.255 = (bf16[256,1024]{1,0:T(8,128)(2,1)S(1)}, bf16[256,1024]{1,0:T(8,128)(2,1)S(1)}, f32[1,1024]{1,0:T(1,128)S(1)}, f32[1,1024]{1,0:T(1,128)S(1)}, f3...) custom-call(bf16[256,1024]{1,0:T(8,128)(2,1)} %tokens_in.1, ...), custom_call_target="tpu_custom_call" | custom-call | tf_op jit(solution)/shard_map/pallas_call | solution.py:983
  226.5 10.8 %shard_map.256 = (bf16[256,1024]{1,0:T(8,128)(2,1)}, bf16[256,1024]{1,0:T(8,128)(2,1)}, f32[1,1024]{1,0:T(1,128)}, f32[1,1024]{1,0:T(1,128)}, f32[1,128]{1,0:T(1...) custom-call(bf16[256,1024]{1,0:T(8,128)(2,1)S(1)} %get-tuple-element, ...), custom_call_target="tpu_custom_call" | custom-call | tf_op jit(solution)/shard_map/pallas_call | solution.py:1040
